TPU v7x, 512 devices: a whole 4x4x16 slice. The times are simulated.
512 devices in a mesh: loop: 16 (over x, y_hi, core), out: 32 (over z, y_lo).
Axes of the slice: x: 4, y: 4 (y_hi: 2, y_lo: 2; y = y_hi * 2 + y_lo), z: 16, core: 2. Of those that a mesh axis runs over, the one named last changes fastest.
Arguments:
- activations: bfloat16 [10, 128, 8192], P(None, 'loop'), may hold values from -6 to 6
- out_grads: bfloat16 [10, 128, 28672], P(None, 'loop', 'out'), may hold values from -6 to 6
- token_counts: int32 [10], replicated, may hold values from 1 to 128, 800 in all
- basis_in: bfloat16 [8192, 8192], P('loop', 'out'), may hold values from -0.0625 to 0.0625
- basis_out: bfloat16 [28672, 14336], P('out', 'loop'), may hold values from -0.03125 to 0.03125
- eigenvalues: float32 [14336, 8192], P('loop', 'out'), may hold values from 0.05 to 5
Outputs:
- scaled_queries: bfloat16 [2, 14336, 8192], P(None, 'loop', 'out')
- scores: float32 [2, 8], replicated
Inputs may be any that keep to these rules, and one draw needn't show every extreme that they name: `token_counts`: the counts sum to exactly 800, and the largest count is exactly 128.
All inputs are finite; a program needn't handle non-finite values.
Results may differ from a plain program's by a relative error of at most 0.0057.
Values may be sent and summed in bfloat16 or wider, within the bound.
A program may use at most 128 MiB of HBM per device.

v0:
```python
import jax
import jax.numpy as jnp
from jax import lax
from jax.sharding import PartitionSpec as P

DIN = 8192
KS = 14336
QUERIES = 2


damping = 0.1


def body(activations, out_grads, token_counts, basis_in, basis_out, eigenvalues):
    examples, rows_here, din = activations.shape
    loop_count = lax.axis_size("loop")
    slots = rows_here * loop_count
    cols_in = basis_in.shape[1]
    cols_out = basis_out.shape[1]
    flat_act = activations.reshape(examples * rows_here, din)
    rotated = jnp.dot(
        flat_act,
        lax.all_gather(basis_in, "loop", axis=0, tiled=True),
        preferred_element_type=jnp.float32,
    )
    rotated = rotated.astype(jnp.bfloat16).reshape(examples, rows_here, cols_in)
    rot_act = lax.all_gather(rotated, "loop", axis=1, tiled=True)
    grads_all = lax.all_gather(out_grads, "loop", axis=1, tiled=True)
    flat_grads = grads_all.reshape(examples * slots, grads_all.shape[2])
    partial_grad = jnp.dot(flat_grads, basis_out, preferred_element_type=jnp.float32)
    rot_rows = lax.psum(partial_grad, "out").astype(jnp.bfloat16)
    positions = jnp.arange(slots, dtype=jnp.int32)
    rot_grad = rot_rows.reshape(examples, slots, cols_out)
    valid = (positions[None, :] < token_counts[:, None]).astype(jnp.bfloat16)
    masked = rot_act * valid[:, :, None]
    factor = 1.0 / slots**0.5
    grad_rot = (
        jnp.einsum("etc,etd->ecd", rot_grad, masked, preferred_element_type=jnp.float32) * factor
    )
    queries = QUERIES
    scaled = (grad_rot[:queries] / (eigenvalues + damping)[None]).astype(jnp.bfloat16)
    partial_scores = jnp.einsum(
        "qcd,fcd->qf",
        scaled.astype(jnp.float32),
        grad_rot[queries:],
        precision=lax.Precision.HIGHEST,
    )
    scores = lax.psum(partial_scores, ("loop", "out")) / (KS * DIN) ** 0.5
    return (scaled, scores)


def solution(mesh):
    return jax.shard_map(
        body,
        mesh=mesh,
        in_specs=(
            P(None, "loop", None),
            P(None, "loop", "out"),
            P(),
            P("loop", "out"),
            P("out", "loop"),
            P("loop", "out"),
        ),
        out_specs=(P(None, "loop", "out"), P()),
        check_vma=False,
    )
```

profile of v0, /device:TPU:1, one launch (start us, length us, event | category | flops | bytes accessed | tf_op | source)
XLA Modules:
  0.0 460.0 jit_solution(11219350362788644562)
XLA Ops:
  7.2 0.0 copy-start
  7.2 0.0 all-gather.3.cloned.1.call-start
  7.2 0.7 all-gather.3.cloned.1.call-update
  7.9 0.0 all-gather.5.cloned.1.call-start
  8.0 0.7 all-gather.5.cloned.1.call-update
  8.7 0.7 fusion.17
  9.4 1.3 broadcast_add_fusion
  10.7 70.9 %all-gather.3.cloned.1.call-done = bf16[10,128,896]{2,1,0:T(8,128)(2,1)} async-done(((bf16[10,8,896]{2,1,0:T(8,128)(2,1)}), bf16[10,128,896]{2,1,0:T(8,128)(2,1)}) %all-gather.3.cloned.1.call-update) | async-done | bytes 2293776 | tf_op jit(solution)/shard_map/all_gather | solution.py:28
  81.5 0.0 copy-done
  81.6 6.5 %fusion.18 = f32[1280,896]{1,0:T(8,128)} fusion(bf16[1280,896]{1,0:T(8,128)(2,1)} %bitcast.18, bf16[896,896]{1,0:T(8,128)(2,1)S(1)} %copy-done), kind=kOutput, calls=%fused_computation.17 | convolution fusion | flops 2055208960 | bytes 8486912 | tf_op jit(solution)/shard_map/dot_general | solution.py:30
  88.1 214.5 %all-reduce.1 = bf16[1280,896]{1,0:T(8,128)(2,1)} all-reduce(f32[1280,896]{1,0:T(8,128)} %fusion.18), channel_id=1, replica_groups=mesh['loop'=16,'out'=32] {'out'}, use_global_device_ids=true, to_apply=%region_0.0 | all-reduce | flops 1146880 | bytes 6881280 | tf_op jit(solution)/shard_map/psum | solution.py:31
  302.6 0.0 all-gather.5.cloned.1.call-done
  302.6 0.0 copy-start.1
  302.6 3.6 fusion.8
  306.1 31.7 %all_gather.11 = bf16[10,128,256]{2,1,0:T(8,128)(2,1)S(1)} all-gather(bf16[10,8,256]{2,1,0:T(8,128)(2,1)S(1)} %fusion.8), channel_id=1, replica_groups=mesh['loop'=16,'out'=32] {'loop'}, dimensions={1}, use_global_device_ids=true | all-gather | bytes 696320 | tf_op jit(solution)/shard_map/all_gather | solution.py:27
  337.8 0.0 copy-done.1
  337.8 1.4 broadcast_multiply_fusion
  339.3 0.5 slice.9
  339.8 0.2 fusion.2
  340.0 0.0 copy-start.2
  340.0 12.0 %fusion.11 = f32[2,8]{1,0:T(2,128)S(1)} fusion(f32[8,896,256]{2,1,0:T(8,128)S(1)} %slice.9, bf16[2,896,256]{2,1,0:T(8,128)(2,1)S(1)} %fusion.2), kind=kOutput, calls=%fused_computation.9 | convolution fusion | flops 44040192 | bytes 8257600 | tf_op jit(solution)/shard_map/qcd,fcd->qf/dot_general | solution.py:42
  352.0 0.0 copy-done.2
  352.0 100.6 %psum.15 = f32[2,8]{1,0:T(2,128)S(1)} all-reduce(f32[2,8]{1,0:T(2,128)S(1)} %fusion.11), channel_id=1, replica_groups=mesh['loop'=16,'out'=32] {'loop','out'}, use_global_device_ids=true, to_apply=%region_1.0 | all-reduce | flops 16 | bytes 128 | tf_op jit(solution)/shard_map/psum | solution.py:48
  452.6 0.6 broadcast_multiply_fusion.1
Async XLA Ops:
  7.2 74.4 %copy-start = (bf16[896,896]{1,0:T(8,128)(2,1)S(1)}, bf16[896,896]{1,0:T(8,128)(2,1)}, u32[]{:S(2)}) copy-start(bf16[896,896]{1,0:T(8,128)(2,1)} %param.10) | copy-start | bytes 4816900
  7.2 74.4 %all-gather.3.cloned.1.call-start = ((), (), s32[]{:S(2)}) async-start(), calls=%async_computation | async-start | bytes 2437120 | tf_op jit(solution)/shard_map/all_gather | solution.py:28
  7.9 294.6 %all-gather.5.cloned.1.call-start = ((), (), s32[]{:S(2)}) async-start(), calls=%async_computation.1 | async-start | bytes 4456448 | tf_op jit(solution)/shard_map/all_gather | solution.py:23
  302.6 35.2 %copy-start.1 = (bf16[1280,896]{1,0:T(8,128)(2,1)S(1)}, bf16[1280,896]{1,0:T(8,128)(2,1)}, u32[]{:S(2)}) copy-start(bf16[1280,896]{1,0:T(8,128)(2,1)} %all-reduce.1) | copy-start | bytes 6881284
  340.0 12.0 %copy-start.2 = (bf16[2,896,256]{2,1,0:T(8,128)(2,1)}, bf16[2,896,256]{2,1,0:T(8,128)(2,1)S(1)}, u32[]{:S(2)}) copy-start(bf16[2,896,256]{2,1,0:T(8,128)(2,1)S(1)} %fusion.2) | copy-start | bytes 2752516
Sparse Core Ops, SparseCore 0:
  11.4 70.1 all-gather.2
  84.8 97.8 all-gather.4
where the time goes:
time: 460 us
  blocking collectives  347 us (75%)
  waiting for transfers between devices  72.3 us (16%)
  matrix products  23.6 us (5%)
  between operations  14.1 us (3%)
    psum x1, blocking collectives, body(): rot_rows = lax.psum(partial_grad, 'out').astype(jnp.bfloat16)  215 us
    psum x1, blocking collectives, body(): scores = lax.psum(partial_scores, ('loop', 'out')) / (KS * DIN) ** 0.5  101 us
    all_gather x1, waiting for transfers between devices, body(): grads_all = lax.all_gather(out_grads, 'loop', axis=1, tiled=True)  70.9 us
    all_gather x1, blocking collectives, body(): rot_act = lax.all_gather(rotated, 'loop', axis=1, tiled=True)  31.7 us
    dot_general x1, matrix products, body(): jnp.einsum('qcd,fcd->qf', scaled.astype(jnp.float32), grad_rot[queries:],...  12 us
  transfers between devices with their start and end apart: 2, of which 1 were waited for; matrix products, arithmetic and copies ran while one was open for 2% of the time, Pallas kernels for 0%

commit v1 on v0

v1 whole, which is shorter than its diff:
```python
import functools

import jax
import jax.numpy as jnp
import numpy as np
from jax import lax
from jax.experimental import pallas as pl
from jax.experimental.pallas import tpu as pltpu
from jax.sharding import PartitionSpec as P

DIN = 8192
KS = 14336
QUERIES = 2
VALID = 800
SUBS = 2
damping = 0.1

F32 = jnp.float32
BF16 = jnp.bfloat16
MESH = pl.DeviceIdType.MESH


def remote(src, dst, send, recv, **where):
    return pltpu.make_async_remote_copy(
        src_ref=src, dst_ref=dst, send_sem=send, recv_sem=recv, device_id=where, device_id_type=MESH
    )


def loop(low, high, body):
    lax.fori_loop(low, high, lambda i, c: (body(i), c)[1], 0)


def kernel(
    d,
    counts, slots, act, grads, basis_in, basis_out, eig,
    scaled_out, scores_out,
    g_all, b_out, onehot, part, rs_first, rs_right, rs_left, y_mine, y_other, rot,
    basis_all, act_all, rot_act, masked, queries, eig_v, scaled, acc, sa, sb,
    loc, g_send, g_recv, f_send, f_recv, b_send, b_recv, a_send, a_recv,
    rs_send, rs_recv, y_send, y_recv, ag_send, ag_recv, ra_send, ra_recv,
    sa_send, sa_recv, sb_send, sb_recv,
):
    L, O, X, Z = d["L"], d["O"], d["X"], d["Z"]
    T, E, rows, CT, QR = d["T"], d["E"], d["rows"], d["CT"], d["QR"]
    CH, SC = d["CH"], d["SC"]
    HR = Z // 2
    HL = Z - 1 - HR
    me_l, me_o = lax.axis_index("loop"), lax.axis_index("out")
    core, yh, x = lax.rem(me_l, 2), lax.rem(me_l // 2, 2), me_l // 4
    z, yl = me_o // 2, lax.rem(me_o, 2)
    partner = me_l + 1 - 2 * core
    y_peer = me_o + 1 - 2 * yl

    def rank(dx, dy, dc):
        return (lax.rem(x + dx, X) * 2 + lax.rem(yh + dy, 2)) * 2 + lax.rem(core + dc, 2)

    def to_loop(r):
        return rank(r // 4, lax.rem(r // 2, 2), lax.rem(r, 2))

    def from_loop(r):
        return rank(X - r // 4, 2 - lax.rem(r // 2, 2), 2 - lax.rem(r, 2))

    def ring(k):
        return lax.rem(z + k + 2 * Z, Z)

    def z_peer(k):
        return ring(k) * 2 + yl

    own_g = pltpu.make_async_copy(grads, g_all.at[me_l], loc.at[0])
    own_act = pltpu.make_async_copy(act, act_all.at[core], loc.at[1])
    own_b = pltpu.make_async_copy(basis_out, b_out, loc.at[2])
    own_eig = pltpu.make_async_copy(eig, eig_v, loc.at[3])
    half = basis_all.shape[2]
    own_basis = pltpu.make_async_copy(
        basis_in.at[:, pl.ds(pl.multiple_of(core * half, half), half)], basis_all.at[me_l], loc.at[4]
    )
    for copy in (own_g, own_b, own_act, own_eig, own_basis):
        copy.start()

    barrier = pltpu.get_barrier_semaphore()
    loop(1, L, lambda r: pl.semaphore_signal(
        barrier, inc=1, device_id={"loop": to_loop(r)}, device_id_type=MESH))
    loop(1, O, lambda k: pl.semaphore_signal(
        barrier, inc=1, device_id={"out": lax.rem(me_o + k, O)}, device_id_type=MESH))
    pl.semaphore_wait(barrier, L + O - 2)

    def g_copy(r):
        return remote(grads, g_all.at[me_l], g_send.at[r], g_recv.at[r], loop=to_loop(2 * r))

    def g_forward(r):
        src = from_loop(2 * r)
        return remote(g_all.at[src], g_all.at[src], f_send.at[r], f_recv.at[r], loop=partner)

    def g_landed(r):
        src = from_loop(2 * r)
        return remote(grads, g_all.at[src], g_send.at[r], g_recv.at[r], loop=partner)

    def g_forwarded(r):
        src = from_loop(2 * r)
        src = src + 1 - 2 * lax.rem(src, 2)
        return remote(grads, g_all.at[src], f_send.at[r], f_recv.at[r], loop=partner)

    shards = L // 2
    loop(1, shards, lambda i: g_copy(shards - i).start())
    remote(grads, g_all.at[me_l], f_send.at[0], f_recv.at[0], loop=partner).start()
    act_copy = remote(act, act_all.at[core], a_send, a_recv, loop=partner)
    act_copy.start()

    which, position = slots[0:1, :], slots[1:2, :]
    target = jnp.full(which.shape, -1, jnp.int32)
    starts = []
    first = jnp.int32(0)
    for e in range(E):
        count = counts[e]
        target = jnp.where((which == e) & (position < count), position + first, target)
        starts.append(first)
        first = first + count
    starts.append(first)
    PB = d["PB"]

    def fill(i):
        at = pl.multiple_of(i * PB, PB)
        row = lax.broadcasted_iota(jnp.int32, (PB, which.shape[1]), 0) + at
        onehot[pl.ds(at, PB), :] = jnp.where(row == target, 1.0, 0.0).astype(BF16)

    loop(0, T // PB, fill)
    if Z * CH > CT * T:
        part[CT * T:, :] = jnp.zeros((Z * CH - CT * T, 128), F32)

    def g_step(r):
        g_landed(r).wait_recv()
        g_forward(r).start()

    loop(1, shards, g_step)

    def basis_copy(r):
        there = lax.rem(core + lax.rem(r, 2), 2)
        return remote(
            basis_in.at[:, pl.ds(pl.multiple_of(there * half, half), half)],
            basis_all.at[me_l], b_send.at[r], b_recv.at[r], loop=to_loop(r))

    def basis_landed(r):
        return remote(basis_all.at[me_l], basis_all.at[from_loop(r)], b_send.at[r], b_recv.at[r], loop=partner)

    loop(1, shards, lambda r: g_copy(r).wait_send())
    loop(1, L, lambda i: basis_copy(L - i).start())

    own_g.wait()
    own_b.wait()
    loop(0, shards, lambda r: g_forwarded(r).wait_recv())

    MB = d["MB"]

    def product(i):
        at = pl.multiple_of(i * MB, MB)
        tall = g_all[...].reshape(L * rows, g_all.shape[2])
        valid = jnp.dot(onehot[pl.ds(at, MB), :], tall, preferred_element_type=F32).astype(BF16)
        y = jnp.dot(valid, b_out[...], preferred_element_type=F32)
        for j in range(CT):
            part[pl.ds(pl.multiple_of(at + j * T, 16), MB), :] = y[:, 128 * j:128 * j + 128]

    loop(0, T // MB, product)

    def rows_of(chunk, u):
        return pl.ds(pl.multiple_of(chunk * CH + u * SC, 16), SC)

    def rs_copy(way, s, u, first=False):
        inbox = rs_right if way == 0 else rs_left
        cut = pl.ds(u * SC, SC)
        source = rs_first.at[way, cut] if first else inbox.at[s - 1, cut]
        k = s * SUBS + u
        return remote(source, inbox.at[s, cut], rs_send.at[way, k], rs_recv.at[way, k],
                      out=z_peer(1 if way == 0 else -1))

    def rs_begin(way, u):
        dest = ring(HR) if way == 0 else ring(-HL)
        rs_first[way, pl.ds(u * SC, SC), :] = part[rows_of(dest, u), :]
        rs_copy(way, 0, u, True).start()

    def rs_step(way, s, u):
        inbox = rs_right if way == 0 else rs_left
        cut = pl.ds(u * SC, SC)
        rs_copy(way, s - 1, u, True).wait_recv()
        dest = ring(HR - s) if way == 0 else ring(s - HL)
        inbox[s - 1, cut, :] = inbox[s - 1, cut, :] + part[rows_of(dest, u), :]
        rs_copy(way, s, u).start()

    for u in range(SUBS):
        rs_begin(0, u)
        if HL:
            rs_begin(1, u)

    def rs_both(s):
        for u in range(SUBS):
            rs_step(0, s, u)
            rs_step(1, s, u)

    loop(1, HL, rs_both)
    for s in range(max(HL, 1), HR):
        for u in range(SUBS):
            rs_step(0, s, u)

    def y_copy(u):
        cut = pl.ds(u * SC, SC)
        return remote(y_mine.at[cut], y_other.at[cut], y_send.at[u], y_recv.at[u], out=y_peer)

    def ag_copy(way, s, u):
        chunk = ring(-s) if way == 0 else ring(s)
        place = rot.at[rows_of(chunk, u)]
        k = s * SUBS + u
        return remote(place, place, ag_send.at[way, k], ag_recv.at[way, k],
                      out=z_peer(1 if way == 0 else -1))

    def ag_landed(way, s, u):
        chunk = ring(-1 - s) if way == 0 else ring(1 + s)
        place = rot.at[rows_of(chunk, u)]
        k = s * SUBS + u
        return remote(place, place, ag_send.at[way, k], ag_recv.at[way, k],
                      out=z_peer(1 if way == 0 else -1))

    for u in range(SUBS):
        cut = pl.ds(u * SC, SC)
        total = part[rows_of(z, u), :]
        if HL:
            rs_copy(1, HL - 1, u, True).wait_recv()
            total = total + rs_left[HL - 1, cut, :]
        rs_copy(0, HR - 1, u, True).wait_recv()
        y_mine[cut, :] = total + rs_right[HR - 1, cut, :]
        y_copy(u).start()
    for u in range(SUBS):
        cut = pl.ds(u * SC, SC)
        y_copy(u).wait_recv()
        rot[rows_of(z, u), :] = (y_mine[cut, :] + y_other[cut, :]).astype(BF16)
        ag_copy(0, 0, u).start()
        if HL:
            ag_copy(1, 0, u).start()

    depth = basis_in.shape[0]
    own_basis.wait()
    own_act.wait()
    act_copy.wait_recv()

    def rotate(r, total):
        src = from_loop(r)

        @pl.when(r > 0)
        def _():
            basis_landed(r).wait_recv()

        a = act_all[:, :, pl.ds(pl.multiple_of(src * depth, depth), depth)].reshape(2 * rows, depth)
        return total + jnp.dot(a, basis_all[src], preferred_element_type=F32)

    def ra_copy(r):
        place = rot_act.at[core, pl.ds(pl.multiple_of((me_l // 2) * 2 * rows, 2 * rows), 2 * rows)]
        return remote(place, place, ra_send.at[r], ra_recv.at[r], loop=to_loop(r))

    def ra_landed(r):
        src = from_loop(r)
        place = rot_act.at[lax.rem(src, 2), pl.ds(pl.multiple_of((src // 2) * 2 * rows, 2 * rows), 2 * rows)]
        return remote(place, place, ra_send.at[r], ra_recv.at[r], loop=partner)

    rotated = jnp.zeros((2 * rows, half), F32)
    for s in range(1, max(HR, 5)):
        if s < 5:
            quarter = L // 4
            rotated = lax.fori_loop((s - 1) * quarter, s * quarter, rotate, rotated)
            if s == 4:
                rot_act[core, pl.ds(pl.multiple_of((me_l // 2) * 2 * rows, 2 * rows), 2 * rows), :] = rotated.astype(BF16)
                loop(1, L, lambda i: ra_copy(L - i).start())
        for u in range(SUBS):
            if s < HR:
                ag_landed(0, s - 1, u).wait_recv()
                ag_copy(0, s, u).start()
            if s < HL:
                ag_landed(1, s - 1, u).wait_recv()
                ag_copy(1, s, u).start()

    loop(1, L, lambda r: ra_landed(r).wait_recv())

    def pick(i):
        at = pl.multiple_of(i * MB, MB)
        for c in range(2):
            masked[pl.ds(at, MB), half * c:half * (c + 1)] = jnp.dot(
                onehot[pl.ds(at, MB), :], rot_act[c], preferred_element_type=F32).astype(BF16)

    loop(0, T // MB, pick)
    row = lax.broadcasted_iota(jnp.int32, (QR, 2 * half), 0)
    top = masked[:QR, :]
    for q in range(QUERIES):
        mine = (row >= starts[q]) & (row < starts[q + 1])
        queries[:, 2 * half * q:2 * half * (q + 1)] = jnp.where(mine, top, jnp.zeros_like(top))
    acc[...] = jnp.zeros_like(acc)
    own_eig.wait()
    for u in range(SUBS):
        if HL:
            ag_landed(1, HL - 1, u).wait_recv()
        ag_landed(0, HR - 1, u).wait_recv()

    factor = 1.0 / d["slots"] ** 0.5
    W = 2 * half

    def finish(j):
        grad = rot[pl.ds(pl.multiple_of(j * T, 16), T), :]
        tile = pl.ds(pl.multiple_of(j * 128, 128), 128)
        outer = lax.dot_general(
            grad[:QR], queries[...], (((0,), (0,)), ((), ())), preferred_element_type=F32) * factor
        divisor = eig_v[tile, :] + damping
        parts = []
        for q in range(QUERIES):
            parts.append((outer[:, W * q:W * (q + 1)] / divisor).astype(BF16))
            scaled[q, tile, :] = parts[q]
        wide = lax.dot_general(
            masked[...], jnp.concatenate(parts, axis=0), (((1,), (1,)), ((), ())), preferred_element_type=F32)
        grad = grad.astype(F32)
        for q in range(QUERIES):
            acc[q] = acc[q] + wide[:, 128 * q:128 * (q + 1)] * grad

    loop(0, CT, finish)
    out_copy = pltpu.make_async_copy(scaled, scaled_out, loc.at[5])
    out_copy.start()

    row = lax.broadcasted_iota(jnp.int32, (T, 128), 0)
    F = E - QUERIES
    for f in range(F):
        mine = (row >= starts[QUERIES + f]) & (row < starts[QUERIES + f + 1])
        for q in range(QUERIES):
            sa[me_l, pl.ds(q * F + f, 1), :] = jnp.sum(jnp.where(mine, acc[q], 0.0), axis=0, keepdims=True)

    def sa_copy(r):
        return remote(sa.at[me_l], sa.at[me_l], sa_send.at[r], sa_recv.at[r], loop=to_loop(r))

    def sa_landed(r):
        src = from_loop(r)
        return remote(sa.at[src], sa.at[src], sa_send.at[r], sa_recv.at[r], loop=partner)

    def sb_copy(k):
        return remote(sb.at[me_o], sb.at[me_o], sb_send.at[k], sb_recv.at[k], out=lax.rem(me_o + k, O))

    def sb_landed(k):
        src = lax.rem(me_o + O - k, O)
        return remote(sb.at[src], sb.at[src], sb_send.at[k], sb_recv.at[k], out=y_peer)

    loop(1, L, lambda r: sa_copy(r).start())
    loop(1, L, lambda r: sa_landed(r).wait_recv())
    sb[me_o] = jnp.sum(sa[...], axis=0)
    loop(1, O, lambda k: sb_copy(k).start())
    loop(1, O, lambda k: sb_landed(k).wait_recv())
    score = jnp.sum(jnp.sum(sb[...], axis=0), axis=1, keepdims=True) * (factor / d["cells"] ** 0.5)
    lane = lax.broadcasted_iota(jnp.int32, (F, F), 1)
    sub = lax.broadcasted_iota(jnp.int32, (F, F), 0)
    for q in range(QUERIES):
        own = jnp.where(lane == sub, score[q * F:(q + 1) * F, :], 0.0)
        scores_out[q:q + 1, :] = jnp.sum(own, axis=0, keepdims=True)

    loop(0, shards, lambda r: g_forward(r).wait_send())
    loop(1, L, lambda r: basis_copy(r).wait_send())
    act_copy.wait_send()
    for way, hops in ((0, HR), (1, HL)):
        for s in range(hops):
            for u in range(SUBS):
                rs_copy(way, s, u, True).wait_send()
                ag_copy(way, s, u).wait_send()
    for u in range(SUBS):
        y_copy(u).wait_send()
    loop(1, L, lambda r: ra_copy(r).wait_send())
    loop(1, L, lambda r: sa_copy(r).wait_send())
    loop(1, O, lambda k: sb_copy(k).wait_send())
    out_copy.wait()


def build(mesh, valid, cells):
    L, O = mesh.shape["loop"], mesh.shape["out"]
    Z = O // 2

    def body(activations, out_grads, token_counts, basis_in, basis_out, eigenvalues):
        E, here, din = activations.shape
        feats, cols = basis_out.shape
        depth, wide = basis_in.shape
        rows = E * here
        slots = here * L
        T, CT = valid, cols // 128
        SC = -(-CT * T // (Z * SUBS * 16)) * 16
        CH = SC * SUBS
        HR = Z // 2
        HL = max(Z - 1 - HR, 1)
        half = wide // 2
        d = dict(L=L, O=O, X=L // 4, Z=Z, T=T, E=E, rows=rows, CT=CT, QR=min(QUERIES * slots, T), CH=CH, SC=SC,
                 PB=80 if T % 80 == 0 else 16, MB=400 if T % 400 == 0 else 16, slots=slots, cells=cells)
        index = np.arange(L * rows)
        table = np.zeros((8, L * rows), np.int32)
        table[0] = index % rows // here
        table[1] = index // rows * here + index % here
        dma = pltpu.SemaphoreType.DMA
        F = E - QUERIES
        scratch = [
            pltpu.VMEM((L, rows, feats), BF16),
            pltpu.VMEM((feats, cols), BF16),
            pltpu.VMEM((T, L * rows), BF16),
            pltpu.VMEM((Z * CH, 128), F32),
            pltpu.VMEM((2, CH, 128), F32),
            pltpu.VMEM((HR, CH, 128), F32),
            pltpu.VMEM((HL, CH, 128), F32),
            pltpu.VMEM((CH, 128), F32),
            pltpu.VMEM((CH, 128), F32),
            pltpu.VMEM((Z * CH, 128), BF16),
            pltpu.VMEM((L, depth, half), BF16),
            pltpu.VMEM((2, rows, din), BF16),
            pltpu.VMEM((2, L * rows, half), BF16),
            pltpu.VMEM((T, wide), BF16),
            pltpu.VMEM((d["QR"], QUERIES * wide), BF16),
            pltpu.VMEM((cols, wide), F32),
            pltpu.VMEM((QUERIES, cols, wide), BF16),
            pltpu.VMEM((QUERIES, T, 128), F32),
            pltpu.VMEM((L, QUERIES * F, 128), F32),
            pltpu.VMEM((O, QUERIES * F, 128), F32),
            dma((6,)),
            dma((L // 2,)), dma((L // 2,)), dma((L // 2,)), dma((L // 2,)),
            dma((L,)), dma((L,)), dma, dma,
            dma((2, HR * SUBS)), dma((2, HR * SUBS)), dma((SUBS,)), dma((SUBS,)),
            dma((2, HR * SUBS)), dma((2, HR * SUBS)),
            dma((L,)), dma((L,)), dma((L,)), dma((L,)), dma((O,)), dma((O,)),
        ]
        hbm = pl.BlockSpec(memory_space=pl.ANY)
        vmem = pl.BlockSpec(memory_space=pltpu.VMEM)
        return pl.pallas_call(
            functools.partial(kernel, d),
            out_shape=(
                jax.ShapeDtypeStruct((QUERIES, cols, wide), BF16),
                jax.ShapeDtypeStruct((QUERIES, F), F32),
            ),
            in_specs=[pl.BlockSpec(memory_space=pltpu.SMEM), vmem, hbm, hbm, hbm, hbm, hbm],
            out_specs=(hbm, vmem),
            scratch_shapes=scratch,
            compiler_params=pltpu.CompilerParams(
                collective_id=0, has_side_effects=True, vmem_limit_bytes=56 * 1024 * 1024),
            cost_estimate=pl.CostEstimate(flops=6 * 10**9, bytes_accessed=6 * 10**6, transcendentals=0),
        )(token_counts, jnp.asarray(table), activations.reshape(rows, din), out_grads.reshape(rows, feats),
          basis_in, basis_out, eigenvalues)

    return jax.shard_map(
        body,
        mesh=mesh,
        in_specs=(
            P(None, "loop", None),
            P(None, "loop", "out"),
            P(),
            P("loop", "out"),
            P("out", "loop"),
            P("loop", "out"),
        ),
        out_specs=(P(None, "loop", "out"), P()),
        check_vma=False,
    )


def solution(mesh):
    return build(mesh, VALID, KS * DIN)
```

time: 460 us -> 141 us (0.31)
  blocking collectives: 347 us -> 0 us
  Pallas kernels: 0 us -> 137 us
  waiting for transfers between devices: 72.3 us -> 0 us
  matrix products: 23.6 us -> 0 us
  between operations: 14.1 us -> 0.65 us
    psum x2 -> x0, blocking collectives: 315 us -> none  [the longest x1 215 us: body(): rot_rows = lax.psum(partial_grad, 'out').astype(jnp.bfloat16)]
    pallas_call x0 -> x1, Pallas kernels: none -> 137 us  [body(): pl.pallas_call(functools.partial(kernel, d), out_shape=(jax.ShapeDtypeStr...]
    all_gather x2 -> x0, waiting for transfers between devices: 70.9 us -> none  [the longest x1 70.9 us: body(): grads_all = lax.all_gather(out_grads, 'loop', axis=1, tiled=True)]
    all_gather x1 -> x0, blocking collectives: 31.7 us -> none  [body(): rot_act = lax.all_gather(rotated, 'loop', axis=1, tiled=True)]
    dot_general x4 -> x0, matrix products: 23.6 us -> none  [the longest x1 12 us: body(): jnp.einsum('qcd,fcd->qf', scaled.astype(jnp.float32), grad_rot[queries:],...]
  transfers between devices with their start and end apart: 2 -> 0, of which waited for: 1 -> 0; matrix products, arithmetic and copies ran while one was open for 2% -> 0% of each run, Pallas kernels for 0% -> 0%
where the time goes in v1:
time: 141 us; the launch traced here: 140 us
  Pallas kernels  137 us (97%)
  local copies, waits for them, and re-layouts  2.73 us (2%)
    pallas_call x1, Pallas kernels, body(): pl.pallas_call(functools.partial(kernel, d), out_shape=(jax.ShapeDtypeStr...  137 us

profile of v1, /device:TPU:1, one launch (start us, length us, event | category | flops | bytes accessed | tf_op | source)
XLA Modules:
  0.0 140.3 jit_solution(12045281579367533315)
XLA Ops:
  0.6 137.0 %shard_map.86 = (bf16[2,896,256]{2,1,0:T(8,128)(2,1)}, f32[2,8]{1,0:T(2,128)}) custom-call(s32[10]{0:T(128)} %counts.1, s32[8,1280]{1,0:T(8,128)} %constant.2.clone.slots, bf16[80,8192]{1,0:T(8,128)(2,1)} %bitcast.2, bf16[80,896]{1,0:T(8,128)(2,1)} %bitcast.3, bf16[512,256]{1,0:T(8,128)(2,1)} %basis_in.1, bf16[896,896]{1,0:T(8,128)(2,1)} %basis_out.1, ...), custom_call_target="tpu_custom_call" | custom-call | flops 6000000000 | bytes 6000000 | tf_op jit(solution)/shard_map/pallas_call | solution.py:425
  137.6 0.0 copy-start
  137.6 2.2 %copy.11 = bf16[2,896,256]{2,1,0:T(8,128)(2,1)} copy(bf16[2,896,256]{2,1,0:T(8,128)(2,1)} %get-tuple-element.4) | data formatting | bytes 1835008
  139.8 0.0 copy-done
  139.8 0.6 copy.12
Async XLA Ops:
  137.6 2.2 %copy-start = (f32[2,8]{1,0:T(2,128)S(1)}, f32[2,8]{1,0:T(2,128)}, u32[]{:S(2)}) copy-start(f32[2,8]{1,0:T(2,128)} %get-tuple-element.5) | copy-start | bytes 196

commit v2 on v1

v2 whole, which is shorter than its diff:
```python
import functools

import jax
import jax.numpy as jnp
import numpy as np
from jax import lax
from jax.experimental import pallas as pl
from jax.experimental.pallas import tpu as pltpu
from jax.sharding import PartitionSpec as P

DIN = 8192
KS = 14336
QUERIES = 2
VALID = 800
PIECES = 4
damping = 0.1

F32 = jnp.float32
BF16 = jnp.bfloat16
MESH = pl.DeviceIdType.MESH


def remote(src, dst, send, recv, **where):
    return pltpu.make_async_remote_copy(
        src_ref=src, dst_ref=dst, send_sem=send, recv_sem=recv, device_id=where, device_id_type=MESH
    )


def loop(low, high, body):
    lax.fori_loop(low, high, lambda i, c: (body(i), c)[1], 0)


def kernel(
    d,
    counts, slots, act, grads, basis_in, basis_out, eig,
    scaled_out, scores_out,
    g_all, b_out, onehot, part, rs_first, rs_right, rs_left, y_mine, y_other, rot,
    basis_all, act_all, rot_act, masked, queries, eig_v, scaled, acc, sa, sb,
    loc, g_send, g_recv, f_send, f_recv, b_send, b_recv, a_send, a_recv,
    rs_send, rs_recv, y_send, y_recv, ag_send, ag_recv, ra_send, ra_recv,
    sa_send, sa_recv, sb_send, sb_recv,
):
    L, O, X, Z = d["L"], d["O"], d["X"], d["Z"]
    T, E, rows, CT, QR = d["T"], d["E"], d["rows"], d["CT"], d["QR"]
    CH, cuts = d["CH"], d["cuts"]
    F = E - QUERIES
    N = len(cuts)
    HR = Z // 2
    HL = Z - 1 - HR
    me_l, me_o = lax.axis_index("loop"), lax.axis_index("out")
    chip, x = me_l // 2, me_l // 4
    core, yh = me_l - 2 * chip, chip - 2 * x
    z = me_o // 2
    yl = me_o - 2 * z
    partner = me_l + 1 - 2 * core
    y_peer = me_o + 1 - 2 * yl

    def wrap(v, n):
        return jnp.where(v >= n, v - n, v)

    xs = [wrap(x + k, X) for k in range(X)]
    ys = [yh, 1 - yh]
    cs = [core, 1 - core]

    def to_loop(r):
        return (xs[r // 4] * 2 + ys[r // 2 % 2]) * 2 + cs[r % 2]

    def from_loop(r):
        return (xs[-(r // 4) % X] * 2 + ys[r // 2 % 2]) * 2 + cs[r % 2]

    def ring(k):
        v = z + k
        return wrap(jnp.where(v < 0, v + Z, v), Z)

    sides = [ring(1) * 2 + yl, ring(-1) * 2 + yl]
    outs = [wrap(me_o + k, O) for k in range(O)]

    own_g = pltpu.make_async_copy(grads, g_all.at[me_l], loc.at[0])
    own_act = pltpu.make_async_copy(act, act_all.at[core], loc.at[1])
    own_b = pltpu.make_async_copy(basis_out, b_out, loc.at[2])
    own_eig = pltpu.make_async_copy(eig, eig_v, loc.at[3])
    half = basis_all.shape[2]

    def columns(c):
        return pl.ds(pl.multiple_of(c * half, half), half)

    own_basis = pltpu.make_async_copy(basis_in.at[:, columns(core)], basis_all.at[me_l], loc.at[4])

    barrier = pltpu.get_barrier_semaphore()
    for r in range(1, L):
        pl.semaphore_signal(barrier, inc=1, device_id={"loop": to_loop(r)}, device_id_type=MESH)
    for k in range(1, O):
        pl.semaphore_signal(barrier, inc=1, device_id={"out": outs[k]}, device_id_type=MESH)
    for copy in (own_g, own_b, own_act, own_eig, own_basis):
        copy.start()
    pl.semaphore_wait(barrier, L + O - 2)

    shards = L // 2

    def g_copy(r):
        return remote(grads, g_all.at[me_l], g_send, g_recv.at[r], loop=to_loop(2 * r))

    def g_landed(r):
        return remote(grads, g_all.at[from_loop(2 * r)], g_send, g_recv.at[r], loop=partner)

    def g_forward(r):
        src = from_loop(2 * r)
        return remote(g_all.at[src], g_all.at[src], f_send, f_recv, loop=partner)

    for r in range(shards - 1, 0, -1):
        g_copy(r).start()
    remote(grads, g_all.at[me_l], f_send, f_recv, loop=partner).start()
    act_copy = remote(act, act_all.at[core], a_send, a_recv, loop=partner)
    act_copy.start()

    which, position = slots[0:1, :], slots[1:2, :]
    target = jnp.full(which.shape, -1, jnp.int32)
    starts = []
    first = jnp.int32(0)
    for e in range(E):
        count = counts[e]
        target = jnp.where((which == e) & (position < count), position + first, target)
        starts.append(first)
        first = first + count
    starts.append(first)
    PB = d["PB"]

    def fill(i):
        at = pl.multiple_of(i * PB, PB)
        row = lax.broadcasted_iota(jnp.int32, (PB, which.shape[1]), 0) + at
        onehot[pl.ds(at, PB), :] = jnp.where(row == target, 1.0, 0.0).astype(BF16)

    loop(0, T // PB, fill)
    if Z * CH > CT * T:
        part[CT * T:, :] = jnp.zeros((Z * CH - CT * T, 128), F32)

    for r in range(1, shards):
        g_landed(r).wait_recv()
        g_forward(r).start()

    def basis_copy(r):
        return remote(basis_in.at[:, columns(cs[r % 2])], basis_all.at[me_l], b_send, b_recv.at[r], loop=to_loop(r))

    def basis_landed(r):
        src = from_loop(r)
        return remote(basis_all.at[src], basis_all.at[src], b_send, b_recv.at[r], loop=partner)

    def whole(ref, send, recv):
        return remote(ref, ref, send, recv, loop=partner)

    g_sent = whole(g_all.at[pl.ds(0, shards - 1)], g_send, g_recv.at[0])
    forwards = whole(g_all.at[pl.ds(0, shards)], f_send, f_recv)
    if shards > 1:
        g_sent.wait_send()
    for r in range(L - 1, 0, -1):
        basis_copy(r).start()

    own_g.wait()
    own_b.wait()
    forwards.wait_recv()

    MB = d["MB"]

    def product(i):
        at = pl.multiple_of(i * MB, MB)
        tall = g_all[...].reshape(L * rows, g_all.shape[2])
        valid = jnp.dot(onehot[pl.ds(at, MB), :], tall, preferred_element_type=F32).astype(BF16)
        y = jnp.dot(valid, b_out[...], preferred_element_type=F32)
        for j in range(CT):
            part[pl.ds(pl.multiple_of(at + j * T, 16), MB), :] = y[:, 128 * j:128 * j + 128]

    loop(0, T // MB, product)

    inboxes = (rs_right, rs_left)

    def rows_of(chunk, u):
        return pl.ds(pl.multiple_of(chunk * CH + cuts[u][0], 16), cuts[u][1])

    def rs_copy(way, s, u):
        cut = pl.ds(*cuts[u])
        source = rs_first.at[way, cut] if s == 0 else inboxes[way].at[s - 1, cut]
        return remote(source, inboxes[way].at[s, cut], rs_send.at[way], rs_recv.at[way, s * N + u], out=sides[way])

    def rs_step(way, s, u):
        cut = pl.ds(*cuts[u])
        dest = rows_of(ring(HR - s) if way == 0 else ring(s - HL), u)
        if s == 0:
            rs_first[way, cut, :] = part[dest, :]
        else:
            rs_copy(way, s - 1, u).wait_recv()
            inboxes[way][s - 1, cut, :] = inboxes[way][s - 1, cut, :] + part[dest, :]
        rs_copy(way, s, u).start()

    depth = basis_in.shape[0]
    order = [0] + list(range(L - 1, 0, -1))
    rotated = [jnp.zeros((2 * rows, half), F32)]

    def rotate():
        r = order.pop(0)
        if r == 0:
            own_basis.wait()
            own_act.wait()
            act_copy.wait_recv()
        else:
            basis_landed(r).wait_recv()
        src = from_loop(r)
        a = act_all[:, :, pl.ds(pl.multiple_of(src * depth, depth), depth)].reshape(2 * rows, depth)
        rotated[0] = rotated[0] + jnp.dot(a, basis_all[src], preferred_element_type=F32)

    def ra_copy(r):
        place = rot_act.at[core * shards + chip]
        return remote(place, place, ra_send, ra_recv, loop=to_loop(r))

    late = max(HR - -(-L // N), 0)
    for s in range(HR):
        for u in range(N):
            rs_step(0, s, u)
            if s < HL:
                rs_step(1, s, u)
            if s >= late and order:
                rotate()
    while order:
        rotate()
    rot_act[core * shards + chip] = rotated[0].astype(BF16)
    for r in range(L - 1, 0, -1):
        ra_copy(r).start()
    rotations = whole(rot_act.at[pl.ds(0, L - 1)], ra_send, ra_recv)

    def y_copy(u):
        cut = pl.ds(*cuts[u])
        return remote(y_mine.at[cut], y_other.at[cut], y_send.at[u], y_recv.at[u], out=y_peer)

    def ag_copy(way, s, u):
        place = rot.at[rows_of(ring(-s) if way == 0 else ring(s), u)]
        return remote(place, place, ag_send.at[way], ag_recv.at[way, s * N + u], out=sides[way])

    def ag_landed(way, s, u):
        place = rot.at[rows_of(ring(-1 - s) if way == 0 else ring(1 + s), u)]
        return remote(place, place, ag_send.at[way], ag_recv.at[way, s * N + u], out=sides[way])

    for u in range(N):
        cut = pl.ds(*cuts[u])
        total = part[rows_of(z, u), :]
        if HL:
            rs_copy(1, HL - 1, u).wait_recv()
            total = total + rs_left[HL - 1, cut, :]
        rs_copy(0, HR - 1, u).wait_recv()
        y_mine[cut, :] = total + rs_right[HR - 1, cut, :]
        y_copy(u).start()
    for u in range(N):
        cut = pl.ds(*cuts[u])
        y_copy(u).wait_recv()
        rot[rows_of(z, u), :] = (y_mine[cut, :] + y_other[cut, :]).astype(BF16)
        ag_copy(0, 0, u).start()
        if HL:
            ag_copy(1, 0, u).start()

    def gather_valid():
        rotations.wait_recv()

        def pick(i):
            at = pl.multiple_of(i * MB, MB)
            for c in range(2):
                panels = rot_act[shards * c:shards * (c + 1)].reshape(L * rows, half)
                masked[pl.ds(at, MB), half * c:half * (c + 1)] = jnp.dot(
                    onehot[pl.ds(at, MB), :], panels, preferred_element_type=F32).astype(BF16)

        loop(0, T // MB, pick)
        row = lax.broadcasted_iota(jnp.int32, (QR, 2 * half), 0)
        top = masked[:QR, :]
        for q in range(QUERIES):
            own = (row >= starts[q]) & (row < starts[q + 1])
            queries[:, 2 * half * q:2 * half * (q + 1)] = jnp.where(own, top, jnp.zeros_like(top))
        acc[...] = jnp.zeros_like(acc)
        own_eig.wait()

    factor = 1.0 / d["slots"] ** 0.5
    W = 2 * half

    def finish(j):
        grad = rot[pl.ds(pl.multiple_of(j * T, 16), T), :]
        tile = pl.ds(pl.multiple_of(j * 128, 128), 128)
        outer = lax.dot_general(
            grad[:QR], queries[...], (((0,), (0,)), ((), ())), preferred_element_type=F32) * factor
        divisor = eig_v[tile, :] + damping
        parts = []
        for q in range(QUERIES):
            parts.append((outer[:, W * q:W * (q + 1)] / divisor).astype(BF16))
            scaled[q, tile, :] = parts[q]
        wide = lax.dot_general(
            masked[...], jnp.concatenate(parts, axis=0), (((1,), (1,)), ((), ())), preferred_element_type=F32)
        grad = grad.astype(F32)
        for q in range(QUERIES):
            acc[q] = acc[q] + wide[:, 128 * q:128 * (q + 1)] * grad

    first_hop = min(3, HR)

    def complete(j):
        low, high = (j * T) // CH, (j * T + T - 1) // CH
        last = jnp.int32(first_hop)
        for k in range((T - 2) // CH + 2):
            chunk = jnp.minimum(low + k, high)
            ahead = chunk - z
            ahead = jnp.where(ahead < 0, ahead + Z, ahead)
            last = jnp.maximum(last, jnp.where(ahead <= HL, ahead, Z - ahead))
        return last

    for s in range(1, HR + 1):
        for u in range(N):
            ag_landed(0, s - 1, u).wait_recv()
            if s < HR:
                ag_copy(0, s, u).start()
            if s <= HL:
                ag_landed(1, s - 1, u).wait_recv()
                if s < HL:
                    ag_copy(1, s, u).start()
        if s == min(2, HR):
            gather_valid()
        if s >= first_hop:

            def ready(j):
                @pl.when(complete(j) == s)
                def _():
                    finish(j)

            loop(0, CT, ready)

    out_copy = pltpu.make_async_copy(scaled, scaled_out, loc.at[5])
    out_copy.start()

    row = lax.broadcasted_iota(jnp.int32, (T, 128), 0)
    lane = lax.broadcasted_iota(jnp.int32, (1, 128), 1)
    mine = [jnp.zeros((1, 128), F32) for q in range(QUERIES)]
    for f in range(F):
        own = (row >= starts[QUERIES + f]) & (row < starts[QUERIES + f + 1])
        for q in range(QUERIES):
            value = jnp.sum(jnp.sum(jnp.where(own, acc[q], 0.0), axis=0, keepdims=True), axis=1, keepdims=True)
            mine[q] = jnp.where(lane == f, value, mine[q])
    for q in range(QUERIES):
        sa[me_l, q:q + 1, :] = mine[q]

    for r in range(L - 1, 0, -1):
        remote(sa.at[me_l], sa.at[me_l], sa_send, sa_recv, loop=to_loop(r)).start()

    forwards.wait_send()
    whole(basis_all.at[pl.ds(0, L - 1)], b_send, b_recv.at[0]).wait_send()
    act_copy.wait_send()
    for way, hops in ((0, HR), (1, HL)):
        if hops:
            whole(inboxes[way].at[pl.ds(0, hops)], rs_send.at[way], rs_recv.at[way, 0]).wait_send()
            whole(rot.at[pl.ds(0, hops * CH)], ag_send.at[way], ag_recv.at[way, 0]).wait_send()
    for u in range(N):
        y_copy(u).wait_send()
    rotations.wait_send()

    sa_all = whole(sa.at[pl.ds(0, L - 1)], sa_send, sa_recv)
    sa_all.wait_recv()
    sb[me_o] = jnp.sum(sa[...], axis=0)
    for k in range(1, O):
        remote(sb.at[me_o], sb.at[me_o], sb_send, sb_recv, out=outs[k]).start()
    sa_all.wait_send()
    out_copy.wait()
    sb_all = whole(sb.at[pl.ds(0, O - 1)], sb_send, sb_recv)
    sb_all.wait_recv()
    total = jnp.sum(sb[...], axis=0) * (factor / d["cells"] ** 0.5)
    scores_out[...] = total[:, :F]
    sb_all.wait_send()


def build(mesh, valid, cells):
    L, O = mesh.shape["loop"], mesh.shape["out"]
    Z = O // 2

    def body(activations, out_grads, token_counts, basis_in, basis_out, eigenvalues):
        E, here, din = activations.shape
        feats, cols = basis_out.shape
        depth, wide = basis_in.shape
        rows = E * here
        slots = here * L
        T, CT = valid, cols // 128
        groups = -(-CT * T // (Z * 16))
        CH = groups * 16
        edges = [groups * u // PIECES * 16 for u in range(PIECES + 1)]
        cuts = [(a, b - a) for a, b in zip(edges, edges[1:]) if b > a]
        N = len(cuts)
        HR = Z // 2
        HL = max(Z - 1 - HR, 1)
        half = wide // 2
        d = dict(L=L, O=O, X=L // 4, Z=Z, T=T, E=E, rows=rows, CT=CT, QR=min(QUERIES * slots, T), CH=CH, cuts=cuts,
                 PB=80 if T % 80 == 0 else 16, MB=400 if T % 400 == 0 else 16, slots=slots, cells=cells)
        index = np.arange(L * rows)
        table = np.zeros((8, L * rows), np.int32)
        table[0] = index % rows // here
        table[1] = index // rows * here + index % here
        dma = pltpu.SemaphoreType.DMA
        F = E - QUERIES
        scratch = [
            pltpu.VMEM((L, rows, feats), BF16),
            pltpu.VMEM((feats, cols), BF16),
            pltpu.VMEM((T, L * rows), BF16),
            pltpu.VMEM((Z * CH, 128), F32),
            pltpu.VMEM((2, CH, 128), F32),
            pltpu.VMEM((HR, CH, 128), F32),
            pltpu.VMEM((HL, CH, 128), F32),
            pltpu.VMEM((CH, 128), F32),
            pltpu.VMEM((CH, 128), F32),
            pltpu.VMEM((Z * CH, 128), BF16),
            pltpu.VMEM((L, depth, half), BF16),
            pltpu.VMEM((2, rows, din), BF16),
            pltpu.VMEM((L, 2 * rows, half), BF16),
            pltpu.VMEM((T, wide), BF16),
            pltpu.VMEM((d["QR"], QUERIES * wide), BF16),
            pltpu.VMEM((cols, wide), F32),
            pltpu.VMEM((QUERIES, cols, wide), BF16),
            pltpu.VMEM((QUERIES, T, 128), F32),
            pltpu.VMEM((L, QUERIES, 128), F32),
            pltpu.VMEM((O, QUERIES, 128), F32),
            dma((6,)),
            dma, dma((L // 2,)), dma, dma,
            dma, dma((L,)), dma, dma,
            dma((2,)), dma((2, HR * N)), dma((N,)), dma((N,)),
            dma((2,)), dma((2, HR * N)),
            dma, dma, dma, dma, dma, dma,
        ]
        hbm = pl.BlockSpec(memory_space=pl.ANY)
        vmem = pl.BlockSpec(memory_space=pltpu.VMEM)
        return pl.pallas_call(
            functools.partial(kernel, d),
            out_shape=(
                jax.ShapeDtypeStruct((QUERIES, cols, wide), BF16),
                jax.ShapeDtypeStruct((QUERIES, F), F32),
            ),
            in_specs=[pl.BlockSpec(memory_space=pltpu.SMEM), vmem, hbm, hbm, hbm, hbm, hbm],
            out_specs=(hbm, vmem),
            scratch_shapes=scratch,
            compiler_params=pltpu.CompilerParams(
                collective_id=0, has_side_effects=True, vmem_limit_bytes=56 * 1024 * 1024),
            cost_estimate=pl.CostEstimate(flops=6 * 10**9, bytes_accessed=6 * 10**6, transcendentals=0),
        )(token_counts, jnp.asarray(table), activations.reshape(rows, din), out_grads.reshape(rows, feats),
          basis_in, basis_out, eigenvalues)

    return jax.shard_map(
        body,
        mesh=mesh,
        in_specs=(
            P(None, "loop", None),
            P(None, "loop", "out"),
            P(),
            P("loop", "out"),
            P("out", "loop"),
            P("loop", "out"),
        ),
        out_specs=(P(None, "loop", "out"), P()),
        check_vma=False,
    )


def solution(mesh):
    return build(mesh, VALID, KS * DIN)
```

time: 141 us -> 128 us (0.908)
  Pallas kernels: 137 us -> 124 us
    pallas_call x1, Pallas kernels: 137 us -> 124 us  [body(): pl.pallas_call(functools.partial(kernel, d), out_shape=(jax.ShapeDtypeStr...]
where the time goes in v2:
time: 128 us; the launch traced here: 127 us
  Pallas kernels  124 us (97%)
  local copies, waits for them, and re-layouts  2.73 us (2%)
    pallas_call x1, Pallas kernels, body(): pl.pallas_call(functools.partial(kernel, d), out_shape=(jax.ShapeDtypeStr...  124 us
    unnamed x4, local copies, waits for them, and re-layouts  2.73 us

profile of v2, /device:TPU:1, one launch (start us, length us, event | category | flops | bytes accessed | tf_op | source)
XLA Modules:
  0.0 127.1 jit_solution(7532145703808978091)
XLA Ops:
  0.6 123.8 %shard_map.86 = (bf16[2,896,256]{2,1,0:T(8,128)(2,1)}, f32[2,8]{1,0:T(2,128)}) custom-call(s32[10]{0:T(128)} %counts.1, s32[8,1280]{1,0:T(8,128)} %constant.2.clone.slots, bf16[80,8192]{1,0:T(8,128)(2,1)} %bitcast.2, bf16[80,896]{1,0:T(8,128)(2,1)} %bitcast.3, bf16[512,256]{1,0:T(8,128)(2,1)} %basis_in.1, bf16[896,896]{1,0:T(8,128)(2,1)} %basis_out.1, ...), custom_call_target="tpu_custom_call" | custom-call | flops 6000000000 | bytes 6000000 | tf_op jit(solution)/shard_map/pallas_call | solution.py:427
  124.4 0.0 copy-start
  124.4 2.2 %copy.11 = bf16[2,896,256]{2,1,0:T(8,128)(2,1)} copy(bf16[2,896,256]{2,1,0:T(8,128)(2,1)} %get-tuple-element.4) | data formatting | bytes 1835008
  126.6 0.0 copy-done
  126.6 0.6 copy.12
Async XLA Ops:
  124.4 2.2 %copy-start = (f32[2,8]{1,0:T(2,128)S(1)}, f32[2,8]{1,0:T(2,128)}, u32[]{:S(2)}) copy-start(f32[2,8]{1,0:T(2,128)} %get-tuple-element.5) | copy-start | bytes 196

commit v3 on v2

--- a/solution.py
+++ b/solution.py
@@ -34,8 +34,8 @@
     d,
     counts, slots, act, grads, basis_in, basis_out, eig,
     scaled_out, scores_out,
-    g_all, b_out, onehot, part, rs_first, rs_right, rs_left, y_mine, y_other, rot,
-    basis_all, act_all, rot_act, masked, queries, eig_v, scaled, acc, sa, sb,
+    g_all, b_out, onehot, valid, part, rs_first, rs_right, rs_left, y_mine, y_other, rot,
+    basis_all, act_all, rot_act, masked, queries, eig_v, acc, sa, sb,
     loc, g_send, g_recv, f_send, f_recv, b_send, b_recv, a_send, a_recv,
     rs_send, rs_recv, y_send, y_recv, ag_send, ag_recv, ra_send, ra_recv,
     sa_send, sa_recv, sb_send, sb_recv,
@@ -89,29 +89,35 @@
     barrier = pltpu.get_barrier_semaphore()
     for r in range(1, L):
         pl.semaphore_signal(barrier, inc=1, device_id={"loop": to_loop(r)}, device_id_type=MESH)
-    for k in range(1, O):
-        pl.semaphore_signal(barrier, inc=1, device_id={"out": outs[k]}, device_id_type=MESH)
+    near = sides + [y_peer]
+    for peer in near:
+        pl.semaphore_signal(barrier, inc=1, device_id={"out": peer}, device_id_type=MESH)
     for copy in (own_g, own_b, own_act, own_eig, own_basis):
         copy.start()
-    pl.semaphore_wait(barrier, L + O - 2)
+    pl.semaphore_wait(barrier, L - 1 + len(near))
 
     shards = L // 2
 
-    def g_copy(r):
-        return remote(grads, g_all.at[me_l], g_send, g_recv.at[r], loop=to_loop(2 * r))
-
-    def g_landed(r):
-        return remote(grads, g_all.at[from_loop(2 * r)], g_send, g_recv.at[r], loop=partner)
-
-    def g_forward(r):
-        src = from_loop(2 * r)
-        return remote(g_all.at[src], g_all.at[src], f_send, f_recv, loop=partner)
-
-    for r in range(shards - 1, 0, -1):
-        g_copy(r).start()
+    low = rows // 32 * 16
+    splits = [(0, low), (low, rows - low)] if low else [(0, rows)]
+    G = len(splits)
+
+    def g_copy(r, p):
+        cut = pl.ds(*splits[p])
+        return remote(grads.at[cut], g_all.at[me_l, cut], g_send, g_recv.at[r, p], loop=to_loop(2 * r))
+
+    def g_landed(r, p):
+        here = g_all.at[from_loop(2 * r), pl.ds(*splits[p])]
+        return remote(here, here, g_send, g_recv.at[r, p], loop=partner)
+
+    def g_forward(r, p):
+        here = g_all.at[from_loop(2 * r), pl.ds(*splits[p])]
+        return remote(here, here, f_send, f_recv, loop=partner)
+
+    for p in range(G):
+        for r in range(shards - 1, 0, -1):
+            g_copy(r, p).start()
     remote(grads, g_all.at[me_l], f_send, f_recv, loop=partner).start()
-    act_copy = remote(act, act_all.at[core], a_send, a_recv, loop=partner)
-    act_copy.start()
 
     which, position = slots[0:1, :], slots[1:2, :]
     target = jnp.full(which.shape, -1, jnp.int32)
@@ -134,9 +140,10 @@
     if Z * CH > CT * T:
         part[CT * T:, :] = jnp.zeros((Z * CH - CT * T, 128), F32)
 
-    for r in range(1, shards):
-        g_landed(r).wait_recv()
-        g_forward(r).start()
+    for p in range(G):
+        for r in range(shards - 1, 0, -1):
+            g_landed(r, p).wait_recv()
+            g_forward(r, p).start()
 
     def basis_copy(r):
         return remote(basis_in.at[:, columns(cs[r % 2])], basis_all.at[me_l], b_send, b_recv.at[r], loop=to_loop(r))
@@ -148,28 +155,55 @@
     def whole(ref, send, recv):
         return remote(ref, ref, send, recv, loop=partner)
 
-    g_sent = whole(g_all.at[pl.ds(0, shards - 1)], g_send, g_recv.at[0])
+    g_sent = whole(g_all.at[pl.ds(0, shards - 1)], g_send, g_recv.at[0, 0])
     forwards = whole(g_all.at[pl.ds(0, shards)], f_send, f_recv)
+    act_copy = remote(act, act_all.at[core], a_send, a_recv, loop=partner)
+    act_copy.start()
     if shards > 1:
         g_sent.wait_send()
     for r in range(L - 1, 0, -1):
         basis_copy(r).start()
-
     own_g.wait()
+    forwards.wait_recv()
+
+    MB = d["MB"]
+
+    def compact(i):
+        cut = pl.ds(pl.multiple_of(i * MB, MB), MB)
+        tall = g_all[...].reshape(L * rows, g_all.shape[2])
+        valid[cut, :] = jnp.dot(onehot[cut, :], tall, preferred_element_type=F32).astype(BF16)
+
+    loop(0, T // MB, compact)
     own_b.wait()
-    forwards.wait_recv()
-
-    MB = d["MB"]
-
-    def product(i):
-        at = pl.multiple_of(i * MB, MB)
-        tall = g_all[...].reshape(L * rows, g_all.shape[2])
-        valid = jnp.dot(onehot[pl.ds(at, MB), :], tall, preferred_element_type=F32).astype(BF16)
-        y = jnp.dot(valid, b_out[...], preferred_element_type=F32)
-        for j in range(CT):
-            part[pl.ds(pl.multiple_of(at + j * T, 16), MB), :] = y[:, 128 * j:128 * j + 128]
-
-    loop(0, T // MB, product)
+
+    def product(j):
+        tile = pl.ds(pl.multiple_of(j * 128, 128), 128)
+
+        def block(i):
+            at = pl.multiple_of(i * MB, MB)
+            part[pl.ds(pl.multiple_of(j * T + at, 16), MB), :] = jnp.dot(
+                valid[pl.ds(at, MB), :], b_out[:, tile], preferred_element_type=F32)
+
+        loop(0, T // MB, block)
+
+    def each_chunk(j, begin, step_of, merge):
+        low, high = (j * T) // CH, (j * T + T - 1) // CH
+        value = jnp.int32(begin)
+        for k in range((T - 2) // CH + 2):
+            ahead = jnp.minimum(low + k, high) - z
+            value = merge(value, step_of(jnp.where(ahead < 0, ahead + Z, ahead)))
+        return value
+
+    def wanted(ahead):
+        return jnp.where(ahead == 0, HR, jnp.where(ahead <= HR, HR - ahead, ahead - HR - 1))
+
+    def products(s):
+        def when_due(j):
+            @pl.when(each_chunk(j, HR, wanted, jnp.minimum) == s)
+            def _():
+                product(j)
+
+        loop(0, CT, when_due)
 
     inboxes = (rs_right, rs_left)
 
@@ -208,23 +242,26 @@
         rotated[0] = rotated[0] + jnp.dot(a, basis_all[src], preferred_element_type=F32)
 
     def ra_copy(r):
-        place = rot_act.at[core * shards + chip]
+        place = rot_act.at[chip, :, columns(core)]
         return remote(place, place, ra_send, ra_recv, loop=to_loop(r))
 
-    late = max(HR - -(-L // N), 0)
+    products(0)
+    late = max(HR - -(-L // (2 * N)), 0)
     for s in range(HR):
         for u in range(N):
             rs_step(0, s, u)
             if s < HL:
                 rs_step(1, s, u)
-            if s >= late and order:
-                rotate()
+            for _ in range(2):
+                if s >= late and order:
+                    rotate()
+        products(s + 1)
     while order:
         rotate()
-    rot_act[core * shards + chip] = rotated[0].astype(BF16)
+    rot_act[chip, :, columns(core)] = rotated[0].astype(BF16)
     for r in range(L - 1, 0, -1):
         ra_copy(r).start()
-    rotations = whole(rot_act.at[pl.ds(0, L - 1)], ra_send, ra_recv)
+    rotations = whole(act_all.at[:, :, pl.ds(0, (L - 1) * half)], ra_send, ra_recv)
 
     def y_copy(u):
         cut = pl.ds(*cuts[u])
@@ -259,11 +296,9 @@
         rotations.wait_recv()
 
         def pick(i):
-            at = pl.multiple_of(i * MB, MB)
-            for c in range(2):
-                panels = rot_act[shards * c:shards * (c + 1)].reshape(L * rows, half)
-                masked[pl.ds(at, MB), half * c:half * (c + 1)] = jnp.dot(
-                    onehot[pl.ds(at, MB), :], panels, preferred_element_type=F32).astype(BF16)
+            cut = pl.ds(pl.multiple_of(i * MB, MB), MB)
+            panels = rot_act[...].reshape(L * rows, 2 * half)
+            masked[cut, :] = jnp.dot(onehot[cut, :], panels, preferred_element_type=F32).astype(BF16)
 
         loop(0, T // MB, pick)
         row = lax.broadcasted_iota(jnp.int32, (QR, 2 * half), 0)
@@ -286,24 +321,17 @@
         parts = []
         for q in range(QUERIES):
             parts.append((outer[:, W * q:W * (q + 1)] / divisor).astype(BF16))
-            scaled[q, tile, :] = parts[q]
+            scaled_out[q, tile, :] = parts[q]
         wide = lax.dot_general(
             masked[...], jnp.concatenate(parts, axis=0), (((1,), (1,)), ((), ())), preferred_element_type=F32)
         grad = grad.astype(F32)
         for q in range(QUERIES):
             acc[q] = acc[q] + wide[:, 128 * q:128 * (q + 1)] * grad
 
-    first_hop = min(3, HR)
-
-    def complete(j):
-        low, high = (j * T) // CH, (j * T + T - 1) // CH
-        last = jnp.int32(first_hop)
-        for k in range((T - 2) // CH + 2):
-            chunk = jnp.minimum(low + k, high)
-            ahead = chunk - z
-            ahead = jnp.where(ahead < 0, ahead + Z, ahead)
-            last = jnp.maximum(last, jnp.where(ahead <= HL, ahead, Z - ahead))
-        return last
+    first_hop = min(4, HR)
+
+    def arrival(ahead):
+        return jnp.where(ahead <= HL, ahead, Z - ahead)
 
     for s in range(1, HR + 1):
         for u in range(N):
@@ -314,19 +342,16 @@
                 ag_landed(1, s - 1, u).wait_recv()
                 if s < HL:
                     ag_copy(1, s, u).start()
-        if s == min(2, HR):
+        if s == min(3, HR):
             gather_valid()
         if s >= first_hop:
 
             def ready(j):
-                @pl.when(complete(j) == s)
+                @pl.when(each_chunk(j, first_hop, arrival, jnp.maximum) == s)
                 def _():
                     finish(j)
 
             loop(0, CT, ready)
-
-    out_copy = pltpu.make_async_copy(scaled, scaled_out, loc.at[5])
-    out_copy.start()
 
     row = lax.broadcasted_iota(jnp.int32, (T, 128), 0)
     lane = lax.broadcasted_iota(jnp.int32, (1, 128), 1)
@@ -359,7 +384,6 @@
     for k in range(1, O):
         remote(sb.at[me_o], sb.at[me_o], sb_send, sb_recv, out=outs[k]).start()
     sa_all.wait_send()
-    out_copy.wait()
     sb_all = whole(sb.at[pl.ds(0, O - 1)], sb_send, sb_recv)
     sb_all.wait_recv()
     total = jnp.sum(sb[...], axis=0) * (factor / d["cells"] ** 0.5)
@@ -398,6 +422,7 @@
             pltpu.VMEM((L, rows, feats), BF16),
             pltpu.VMEM((feats, cols), BF16),
             pltpu.VMEM((T, L * rows), BF16),
+            pltpu.VMEM((T, feats), BF16),
             pltpu.VMEM((Z * CH, 128), F32),
             pltpu.VMEM((2, CH, 128), F32),
             pltpu.VMEM((HR, CH, 128), F32),
@@ -407,16 +432,15 @@
             pltpu.VMEM((Z * CH, 128), BF16),
             pltpu.VMEM((L, depth, half), BF16),
             pltpu.VMEM((2, rows, din), BF16),
-            pltpu.VMEM((L, 2 * rows, half), BF16),
+            pltpu.VMEM((L // 2, 2 * rows, wide), BF16),
             pltpu.VMEM((T, wide), BF16),
             pltpu.VMEM((d["QR"], QUERIES * wide), BF16),
             pltpu.VMEM((cols, wide), F32),
-            pltpu.VMEM((QUERIES, cols, wide), BF16),
             pltpu.VMEM((QUERIES, T, 128), F32),
             pltpu.VMEM((L, QUERIES, 128), F32),
             pltpu.VMEM((O, QUERIES, 128), F32),
-            dma((6,)),
-            dma, dma((L // 2,)), dma, dma,
+            dma((5,)),
+            dma, dma((L // 2, 2)), dma, dma,
             dma, dma((L,)), dma, dma,
             dma((2,)), dma((2, HR * N)), dma((N,)), dma((N,)),
             dma((2,)), dma((2, HR * N)),
@@ -427,11 +451,11 @@
         return pl.pallas_call(
             functools.partial(kernel, d),
             out_shape=(
-                jax.ShapeDtypeStruct((QUERIES, cols, wide), BF16),
-                jax.ShapeDtypeStruct((QUERIES, F), F32),
+                pltpu.VMEM((QUERIES, cols, wide), BF16),
+                pltpu.VMEM((QUERIES, F), F32),
             ),
             in_specs=[pl.BlockSpec(memory_space=pltpu.SMEM), vmem, hbm, hbm, hbm, hbm, hbm],
-            out_specs=(hbm, vmem),
+            out_specs=(vmem, vmem),
             scratch_shapes=scratch,
             compiler_params=pltpu.CompilerParams(
                 collective_id=0, has_side_effects=True, vmem_limit_bytes=56 * 1024 * 1024),

time: 128 us -> 123 us (0.961)
  Pallas kernels: 124 us -> 120 us
    pallas_call x1, Pallas kernels: 124 us -> 120 us  [body(): pl.pallas_call(functools.partial(kernel, d), out_shape=(pltpu.VMEM((QUERI...]
    unnamed x4 -> x2, local copies, waits for them, and re-layouts: 2.73 us -> 1.49 us
where the time goes in v3:
time: 123 us
  Pallas kernels  120 us (98%)
  local copies, waits for them, and re-layouts  1.49 us (1%)
    pallas_call x1, Pallas kernels, body(): pl.pallas_call(functools.partial(kernel, d), out_shape=(pltpu.VMEM((QUERI...  120 us

profile of v3, /device:TPU:1, one launch (start us, length us, event | category | flops | bytes accessed | tf_op | source)
XLA Modules:
  0.0 122.6 jit_solution(10664349029011780670)
XLA Ops:
  0.6 120.5 %shard_map.86 = (bf16[2,896,256]{2,1,0:T(8,128)(2,1)S(1)}, f32[2,8]{1,0:T(2,128)S(1)}) custom-call(s32[10]{0:T(128)} %counts.1, s32[8,1280]{1,0:T(8,128)} %constant.2.clone.slots, bf16[80,8192]{1,0:T(8,128)(2,1)} %bitcast.2, bf16[80,896]{1,0:T(8,128)(2,1)} %bitcast.3, bf16[512,256]{1,0:T(8,128)(2,1)} %basis_in.1, bf16[896,896]{1,0:T(8,128)(2,1)} %basis_out.1, ...), custom_call_target="tpu_custom_call" | custom-call | flops 6000000000 | bytes 6000000 | tf_op jit(solution)/shard_map/pallas_call | solution.py:451
  121.1 0.9 copy.11
  122.1 0.6 copy.12

commit v4 on v3

--- a/solution.py
+++ b/solution.py
@@ -252,15 +252,9 @@
             rs_step(0, s, u)
             if s < HL:
                 rs_step(1, s, u)
-            for _ in range(2):
-                if s >= late and order:
-                    rotate()
+            if s >= late and order:
+                rotate()
         products(s + 1)
-    while order:
-        rotate()
-    rot_act[chip, :, columns(core)] = rotated[0].astype(BF16)
-    for r in range(L - 1, 0, -1):
-        ra_copy(r).start()
     rotations = whole(act_all.at[:, :, pl.ds(0, (L - 1) * half)], ra_send, ra_recv)
 
     def y_copy(u):
@@ -284,6 +278,8 @@
         rs_copy(0, HR - 1, u).wait_recv()
         y_mine[cut, :] = total + rs_right[HR - 1, cut, :]
         y_copy(u).start()
+    while order:
+        rotate()
     for u in range(N):
         cut = pl.ds(*cuts[u])
         y_copy(u).wait_recv()
@@ -291,6 +287,9 @@
         ag_copy(0, 0, u).start()
         if HL:
             ag_copy(1, 0, u).start()
+    rot_act[chip, :, columns(core)] = rotated[0].astype(BF16)
+    for r in range(L - 1, 0, -1):
+        ra_copy(r).start()
 
     def gather_valid():
         rotations.wait_recv()

time: 123 us -> 120 us (0.976)
  Pallas kernels: 120 us -> 117 us
    pallas_call x1, Pallas kernels: 120 us -> 117 us  [body(): pl.pallas_call(functools.partial(kernel, d), out_shape=(pltpu.VMEM((QUERI...]
where the time goes in v4:
time: 120 us; the launch traced here: 119 us
  Pallas kernels  117 us (98%)
  local copies, waits for them, and re-layouts  1.49 us (1%)
    pallas_call x1, Pallas kernels, body(): pl.pallas_call(functools.partial(kernel, d), out_shape=(pltpu.VMEM((QUERI...  117 us

profile of v4, /device:TPU:1, one launch (start us, length us, event | category | flops | bytes accessed | tf_op | source)
XLA Modules:
  0.0 119.2 jit_solution(886098452316887711)
XLA Ops:
  0.6 117.1 %shard_map.86 = (bf16[2,896,256]{2,1,0:T(8,128)(2,1)S(1)}, f32[2,8]{1,0:T(2,128)S(1)}) custom-call(s32[10]{0:T(128)} %counts.1, s32[8,1280]{1,0:T(8,128)} %constant.2.clone.slots, bf16[80,8192]{1,0:T(8,128)(2,1)} %bitcast.2, bf16[80,896]{1,0:T(8,128)(2,1)} %bitcast.3, bf16[512,256]{1,0:T(8,128)(2,1)} %basis_in.1, bf16[896,896]{1,0:T(8,128)(2,1)} %basis_out.1, ...), custom_call_target="tpu_custom_call" | custom-call | flops 6000000000 | bytes 6000000 | tf_op jit(solution)/shard_map/pallas_call | solution.py:450
  117.7 0.9 copy.11
  118.6 0.6 copy.12

commit v5 on v4

--- a/solution.py
+++ b/solution.py
@@ -34,7 +34,7 @@
     d,
     counts, slots, act, grads, basis_in, basis_out, eig,
     scaled_out, scores_out,
-    g_all, b_out, onehot, valid, part, rs_first, rs_right, rs_left, y_mine, y_other, rot,
+    g_first, g_second, b_out, onehot, valid, part, rs_right, rs_left, y_mine, y_other, rot,
     basis_all, act_all, rot_act, masked, queries, eig_v, acc, sa, sb,
     loc, g_send, g_recv, f_send, f_recv, b_send, b_recv, a_send, a_recv,
     rs_send, rs_recv, y_send, y_recv, ag_send, ag_recv, ra_send, ra_recv,
@@ -75,7 +75,11 @@
     sides = [ring(1) * 2 + yl, ring(-1) * 2 + yl]
     outs = [wrap(me_o + k, O) for k in range(O)]
 
-    own_g = pltpu.make_async_copy(grads, g_all.at[me_l], loc.at[0])
+    splits = d["splits"]
+    boxes = (g_first, g_second)
+    own_g = [
+        pltpu.make_async_copy(grads.at[pl.ds(*splits[p])], boxes[p].at[me_l], loc.at[5 * p]) for p in range(2)
+    ]
     own_act = pltpu.make_async_copy(act, act_all.at[core], loc.at[1])
     own_b = pltpu.make_async_copy(basis_out, b_out, loc.at[2])
     own_eig = pltpu.make_async_copy(eig, eig_v, loc.at[3])
@@ -92,32 +96,28 @@
     near = sides + [y_peer]
     for peer in near:
         pl.semaphore_signal(barrier, inc=1, device_id={"out": peer}, device_id_type=MESH)
-    for copy in (own_g, own_b, own_act, own_eig, own_basis):
+    for copy in (*own_g, own_b, own_act, own_eig, own_basis):
         copy.start()
     pl.semaphore_wait(barrier, L - 1 + len(near))
 
     shards = L // 2
 
-    low = rows // 32 * 16
-    splits = [(0, low), (low, rows - low)] if low else [(0, rows)]
-    G = len(splits)
-
     def g_copy(r, p):
         cut = pl.ds(*splits[p])
-        return remote(grads.at[cut], g_all.at[me_l, cut], g_send, g_recv.at[r, p], loop=to_loop(2 * r))
+        return remote(grads.at[cut], boxes[p].at[me_l], g_send, g_recv.at[r, p], loop=to_loop(2 * r))
 
     def g_landed(r, p):
-        here = g_all.at[from_loop(2 * r), pl.ds(*splits[p])]
+        here = boxes[p].at[from_loop(2 * r)]
         return remote(here, here, g_send, g_recv.at[r, p], loop=partner)
 
     def g_forward(r, p):
-        here = g_all.at[from_loop(2 * r), pl.ds(*splits[p])]
-        return remote(here, here, f_send, f_recv, loop=partner)
-
-    for p in range(G):
+        here = boxes[p].at[from_loop(2 * r)]
+        return remote(here, here, f_send, f_recv.at[p], loop=partner)
+
+    for p in range(2):
         for r in range(shards - 1, 0, -1):
             g_copy(r, p).start()
-    remote(grads, g_all.at[me_l], f_send, f_recv, loop=partner).start()
+        remote(grads.at[pl.ds(*splits[p])], boxes[p].at[me_l], f_send, f_recv.at[p], loop=partner).start()
 
     which, position = slots[0:1, :], slots[1:2, :]
     target = jnp.full(which.shape, -1, jnp.int32)
@@ -140,7 +140,7 @@
     if Z * CH > CT * T:
         part[CT * T:, :] = jnp.zeros((Z * CH - CT * T, 128), F32)
 
-    for p in range(G):
+    for p in range(2):
         for r in range(shards - 1, 0, -1):
             g_landed(r, p).wait_recv()
             g_forward(r, p).start()
@@ -155,25 +155,29 @@
     def whole(ref, send, recv):
         return remote(ref, ref, send, recv, loop=partner)
 
-    g_sent = whole(g_all.at[pl.ds(0, shards - 1)], g_send, g_recv.at[0, 0])
-    forwards = whole(g_all.at[pl.ds(0, shards)], f_send, f_recv)
+    g_sent = whole(valid.at[pl.ds(0, rows * (shards - 1))], g_send, g_recv.at[0, 0])
+    g_forwards_sent = whole(valid.at[pl.ds(0, rows * shards)], f_send, f_recv.at[0])
     act_copy = remote(act, act_all.at[core], a_send, a_recv, loop=partner)
     act_copy.start()
     if shards > 1:
         g_sent.wait_send()
     for r in range(L - 1, 0, -1):
         basis_copy(r).start()
-    own_g.wait()
-    forwards.wait_recv()
 
     MB = d["MB"]
-
-    def compact(i):
-        cut = pl.ds(pl.multiple_of(i * MB, MB), MB)
-        tall = g_all[...].reshape(L * rows, g_all.shape[2])
-        valid[cut, :] = jnp.dot(onehot[cut, :], tall, preferred_element_type=F32).astype(BF16)
-
-    loop(0, T // MB, compact)
+    edge = L * splits[0][1]
+    for p in range(2):
+        own_g[p].wait()
+        whole(boxes[p].at[pl.ds(0, shards)], f_send, f_recv.at[p]).wait_recv()
+
+        def compact(i):
+            cut = pl.ds(pl.multiple_of(i * MB, MB), MB)
+            tall = boxes[p][...].reshape(L * splits[p][1], grads.shape[1])
+            chosen = onehot[cut, edge:] if p else onehot[cut, :edge]
+            moved = jnp.dot(chosen, tall, preferred_element_type=F32).astype(BF16)
+            valid[cut, :] = valid[cut, :] + moved if p else moved
+
+        loop(0, T // MB, compact)
     own_b.wait()
 
     def product(j):
@@ -212,15 +216,13 @@
 
     def rs_copy(way, s, u):
         cut = pl.ds(*cuts[u])
-        source = rs_first.at[way, cut] if s == 0 else inboxes[way].at[s - 1, cut]
+        source = inboxes[way].at[s - 1, cut] if s else part.at[rows_of(ring(HR) if way == 0 else ring(-HL), u)]
         return remote(source, inboxes[way].at[s, cut], rs_send.at[way], rs_recv.at[way, s * N + u], out=sides[way])
 
     def rs_step(way, s, u):
         cut = pl.ds(*cuts[u])
         dest = rows_of(ring(HR - s) if way == 0 else ring(s - HL), u)
-        if s == 0:
-            rs_first[way, cut, :] = part[dest, :]
-        else:
+        if s:
             rs_copy(way, s - 1, u).wait_recv()
             inboxes[way][s - 1, cut, :] = inboxes[way][s - 1, cut, :] + part[dest, :]
         rs_copy(way, s, u).start()
@@ -296,8 +298,11 @@
 
         def pick(i):
             cut = pl.ds(pl.multiple_of(i * MB, MB), MB)
-            panels = rot_act[...].reshape(L * rows, 2 * half)
-            masked[cut, :] = jnp.dot(onehot[cut, :], panels, preferred_element_type=F32).astype(BF16)
+            panels = rot_act[...].reshape(L, rows, 2 * half)
+            pieces = [panels[:, a:a + n].reshape(L * n, 2 * half) for a, n in splits]
+            total = jnp.dot(onehot[cut, :edge], pieces[0], preferred_element_type=F32)
+            total = total + jnp.dot(onehot[cut, edge:], pieces[1], preferred_element_type=F32)
+            masked[cut, :] = total.astype(BF16)
 
         loop(0, T // MB, pick)
         row = lax.broadcasted_iota(jnp.int32, (QR, 2 * half), 0)
@@ -363,10 +368,10 @@
     for q in range(QUERIES):
         sa[me_l, q:q + 1, :] = mine[q]
 
-    for r in range(L - 1, 0, -1):
+    for r in sorted(range(1, L), key=lambda r: -min(r // 4, X - r // 4) - r // 2 % 2 * 2):
         remote(sa.at[me_l], sa.at[me_l], sa_send, sa_recv, loop=to_loop(r)).start()
 
-    forwards.wait_send()
+    g_forwards_sent.wait_send()
     whole(basis_all.at[pl.ds(0, L - 1)], b_send, b_recv.at[0]).wait_send()
     act_copy.wait_send()
     for way, hops in ((0, HR), (1, HL)):
@@ -380,7 +385,7 @@
     sa_all = whole(sa.at[pl.ds(0, L - 1)], sa_send, sa_recv)
     sa_all.wait_recv()
     sb[me_o] = jnp.sum(sa[...], axis=0)
-    for k in range(1, O):
+    for k in sorted(range(1, O), key=lambda k: -min(k, O - k)):
         remote(sb.at[me_o], sb.at[me_o], sb_send, sb_recv, out=outs[k]).start()
     sa_all.wait_send()
     sb_all = whole(sb.at[pl.ds(0, O - 1)], sb_send, sb_recv)
@@ -409,21 +414,24 @@
         HR = Z // 2
         HL = max(Z - 1 - HR, 1)
         half = wide // 2
-        d = dict(L=L, O=O, X=L // 4, Z=Z, T=T, E=E, rows=rows, CT=CT, QR=min(QUERIES * slots, T), CH=CH, cuts=cuts,
-                 PB=80 if T % 80 == 0 else 16, MB=400 if T % 400 == 0 else 16, slots=slots, cells=cells)
         index = np.arange(L * rows)
+        low = -(-rows // 32) * 16
+        splits = [(0, low), (low, rows - low)]
+        index = np.concatenate([index.reshape(L, rows)[:, a:a + n].ravel() for a, n in splits])
         table = np.zeros((8, L * rows), np.int32)
         table[0] = index % rows // here
         table[1] = index // rows * here + index % here
+        d = dict(splits=splits, L=L, O=O, X=L // 4, Z=Z, T=T, E=E, rows=rows, CT=CT, QR=min(QUERIES * slots, T), CH=CH, cuts=cuts,
+                 PB=80 if T % 80 == 0 else 16, MB=400 if T % 400 == 0 else 16, slots=slots, cells=cells)
         dma = pltpu.SemaphoreType.DMA
         F = E - QUERIES
         scratch = [
-            pltpu.VMEM((L, rows, feats), BF16),
+            pltpu.VMEM((L, low, feats), BF16),
+            pltpu.VMEM((L, rows - low, feats), BF16),
             pltpu.VMEM((feats, cols), BF16),
             pltpu.VMEM((T, L * rows), BF16),
             pltpu.VMEM((T, feats), BF16),
             pltpu.VMEM((Z * CH, 128), F32),
-            pltpu.VMEM((2, CH, 128), F32),
             pltpu.VMEM((HR, CH, 128), F32),
             pltpu.VMEM((HL, CH, 128), F32),
             pltpu.VMEM((CH, 128), F32),
@@ -438,8 +446,8 @@
             pltpu.VMEM((QUERIES, T, 128), F32),
             pltpu.VMEM((L, QUERIES, 128), F32),
             pltpu.VMEM((O, QUERIES, 128), F32),
-            dma((5,)),
-            dma, dma((L // 2, 2)), dma, dma,
+            dma((6,)),
+            dma, dma((L // 2, 2)), dma, dma((2,)),
             dma, dma((L,)), dma, dma,
             dma((2,)), dma((2, HR * N)), dma((N,)), dma((N,)),
             dma((2,)), dma((2, HR * N)),

time: 120 us -> 119 us (level)
  no operation moved by 1% of the time
where the time goes in v5:
time: 119 us
  Pallas kernels  117 us (98%)
  local copies, waits for them, and re-layouts  1.49 us (1%)
    pallas_call x1, Pallas kernels, body(): pl.pallas_call(functools.partial(kernel, d), out_shape=(pltpu.VMEM((QUERI...  117 us

profile of v5, /device:TPU:1, one launch (start us, length us, event | category | flops | bytes accessed | tf_op | source)
XLA Modules:
  0.0 119.1 jit_solution(8710195641731923241)
XLA Ops:
  0.6 116.9 %shard_map.86 = (bf16[2,896,256]{2,1,0:T(8,128)(2,1)S(1)}, f32[2,8]{1,0:T(2,128)S(1)}) custom-call(s32[10]{0:T(128)} %counts.1, s32[8,1280]{1,0:T(8,128)} %constant.2.clone.slots, bf16[80,8192]{1,0:T(8,128)(2,1)} %bitcast.2, bf16[80,896]{1,0:T(8,128)(2,1)} %bitcast.3, bf16[512,256]{1,0:T(8,128)(2,1)} %basis_in.1, bf16[896,896]{1,0:T(8,128)(2,1)} %basis_out.1, ...), custom_call_target="tpu_custom_call" | custom-call | flops 6000000000 | bytes 6000000 | tf_op jit(solution)/shard_map/pallas_call | solution.py:458
  117.6 0.9 copy.11
  118.5 0.6 copy.12

commit v6 on v5

--- a/solution.py
+++ b/solution.py
@@ -158,7 +158,6 @@
     g_sent = whole(valid.at[pl.ds(0, rows * (shards - 1))], g_send, g_recv.at[0, 0])
     g_forwards_sent = whole(valid.at[pl.ds(0, rows * shards)], f_send, f_recv.at[0])
     act_copy = remote(act, act_all.at[core], a_send, a_recv, loop=partner)
-    act_copy.start()
     if shards > 1:
         g_sent.wait_send()
     for r in range(L - 1, 0, -1):
@@ -178,6 +177,7 @@
             valid[cut, :] = valid[cut, :] + moved if p else moved
 
         loop(0, T // MB, compact)
+    act_copy.start()
     own_b.wait()
 
     def product(j):

time: 119 us -> 119 us (level)
  no operation moved by 1% of the time
where the time goes in v6:
time: 119 us
  Pallas kernels  117 us (98%)
  local copies, waits for them, and re-layouts  1.49 us (1%)
    pallas_call x1, Pallas kernels, body(): pl.pallas_call(functools.partial(kernel, d), out_shape=(pltpu.VMEM((QUERI...  117 us

profile of v6, /device:TPU:1, one launch (start us, length us, event | category | flops | bytes accessed | tf_op | source)
XLA Modules:
  0.0 119.1 jit_solution(17250933123384196005)
XLA Ops:
  0.6 116.9 %shard_map.86 = (bf16[2,896,256]{2,1,0:T(8,128)(2,1)S(1)}, f32[2,8]{1,0:T(2,128)S(1)}) custom-call(s32[10]{0:T(128)} %counts.1, s32[8,1280]{1,0:T(8,128)} %constant.2.clone.slots, bf16[80,8192]{1,0:T(8,128)(2,1)} %bitcast.2, bf16[80,896]{1,0:T(8,128)(2,1)} %bitcast.3, bf16[512,256]{1,0:T(8,128)(2,1)} %basis_in.1, bf16[896,896]{1,0:T(8,128)(2,1)} %basis_out.1, ...), custom_call_target="tpu_custom_call" | custom-call | flops 6000000000 | bytes 6000000 | tf_op jit(solution)/shard_map/pallas_call | solution.py:458
  117.6 0.9 copy.11
  118.5 0.6 copy.12
